TPU v7x, 32 devices: a whole 2x2x4 slice. The times are simulated.
32 devices in a mesh: parts: 2 (over y), wide: 4 (over x, core), narrow: 4 (over z).
Axes of the slice: x: 2, y: 2, z: 4, core: 2. Of those that a mesh axis runs over, the one named last changes fastest.
Arguments:
- cand_grads: bfloat16 [1280, 16384], P(('parts', 'wide'), 'narrow'), parts along dimension 0, may hold values from -6 to 6
- train_feats: bfloat16 [1024, 16384], P(('parts', 'wide'), 'narrow'), parts along dimension 0, may hold values from -0.046875 to 0.046875
- span_ids: int32 [1024], P('parts'), parts along dimension 0, may hold values from 0 to 63, never falling along the last dimension, each value on 1 to 32 neighbouring positions
- group_ids: int32 [1280], P(('parts', 'wide')), parts along dimension 0, may hold values from 0 to 39, as said below
- eig_values: float32 [128, 128], replicated, may hold values from 0.05 to 2
- input_basis: float32 [128, 128], replicated, may hold values from -0.5 to 0.5
- basis: float32 [128, 128], replicated, may hold values from -0.5 to 0.5
Outputs:
- doc_influence: float32 [1280, 64], P(('parts', 'wide'), 'narrow'), parts along dimension 0
There are 2 independent parts, one for each index of `parts`. A program takes and returns all parts, laid end to end along the dimension named above; an argument that names none is the same for every part. Nothing has to cross between parts.
Inputs may be any that keep to these rules, and one draw needn't show every extreme that they name: `group_ids`: each prompt id names exactly 16 candidates. `span_ids`: never falls along the training rows, and every document has at least one row.
All inputs are finite; a program needn't handle non-finite values.
Results may differ from a plain program's by a relative error of at most 0.0042.
Values may be sent and summed in bfloat16 or wider, within the bound.
A program may use at most 64 MiB of HBM per device.

v0:
```python
import jax
import jax.numpy as jnp
from jax import lax
from jax.sharding import PartitionSpec as P

DOCS_DEV = 16
NBEST = 16


damping = 0.05
lowest = -1e30


def shifted(value, axis, steps):
    count = lax.axis_size(axis)
    pairs = [(source, (source + steps) % count) for source in range(count)]
    return lax.ppermute(value, axis, pairs)


def keep_peak(earlier, following):
    peak_value = jnp.where(following[1], following[0], jnp.maximum(earlier[0], following[0]))
    return (peak_value, earlier[1] | following[1])


def segment_peaks(score_rows, row_docs, wanted):
    row_count = row_docs.shape[0]
    change = row_docs[1:] != row_docs[:-1]
    segment_start = jnp.concatenate([jnp.ones((1,), jnp.bool_), change])
    starts_wide = jnp.broadcast_to(segment_start[None, :], score_rows.shape)
    running, unused = lax.associative_scan(keep_peak, (score_rows, starts_wide), axis=1)
    last_row = jnp.sum((row_docs[:, None] <= wanted[None, :]).astype(jnp.int32), axis=0) - 1
    safe_row = jnp.clip(last_row, 0, row_count - 1)
    picked = jnp.take(running, safe_row, axis=1)
    present = (last_row >= 0) & (row_docs[safe_row] == wanted)
    return jnp.where(present[None, :], picked, lowest)


def local(cand_grads, train_feats, span_ids, group_ids, eig_values, input_basis, basis):
    highest = lax.Precision.HIGHEST
    cand_rows, width = cand_grads.shape
    block_rows = train_feats.shape[0]
    in_rows, out_cols = eig_values.shape
    wide_count = lax.axis_size("wide")
    narrow_count = lax.axis_size("narrow")
    doc_count = DOCS_DEV * wide_count
    position = lax.axis_index("wide")
    local_in = in_rows // narrow_count
    per_peer = cand_rows // narrow_count
    gradient_pieces = cand_grads.reshape(narrow_count, per_peer, local_in, out_cols)
    gradients = lax.all_to_all(gradient_pieces, "narrow", split_axis=0, concat_axis=2, tiled=True)[
        0
    ].astype(jnp.float32)
    left_side = jnp.einsum("nab,bc->nac", gradients, basis, precision=highest)
    rotated = jnp.einsum("ae,nac->nec", input_basis, left_side, precision=highest)
    scaled = rotated / (eig_values + damping)
    right_side = jnp.einsum("nec,bc->neb", scaled, basis, precision=highest)
    restored = jnp.einsum("ae,neb->nab", input_basis, right_side, precision=highest)
    rounded = restored.astype(jnp.bfloat16)[None]
    returned = lax.all_to_all(rounded, "narrow", split_axis=2, concat_axis=0, tiled=True)
    precond = returned.reshape(cand_rows, width)

    def add_block(score_tile, train_block, anchor):
        partial_value = lax.dot_general(
            precond, train_block, (((1,), (1,)), ((), ())), preferred_element_type=jnp.float32
        )
        return lax.dynamic_update_slice_in_dim(score_tile, partial_value, anchor * block_rows, 1)

    blank_tile = jnp.zeros((cand_rows, block_rows * wide_count), jnp.float32)
    score_tile = add_block(blank_tile, train_feats, position)

    def advance(turn_index, carried):
        train_block, tile_now = carried
        train_block = shifted(train_block, "wide", 1)
        return (train_block, add_block(tile_now, train_block, (position - turn_index) % wide_count))

    unused, score_tile = lax.fori_loop(1, wide_count, advance, (train_feats, score_tile))
    doc_share = doc_count // narrow_count
    offset = lax.axis_index("narrow") * doc_share
    summed = lax.psum(score_tile, "narrow")
    wanted = offset + jnp.arange(doc_share, dtype=jnp.int32)
    doc_peak = segment_peaks(summed, span_ids, wanted)
    group_count = cand_rows * wide_count // NBEST
    member = (group_ids[:, None] == jnp.arange(group_count, dtype=jnp.int32)[None, :]).astype(
        jnp.float32
    )
    local_groups = lax.dot_general(member, doc_peak, (((0,), (0,)), ((), ())), precision=highest)
    group_mean = lax.psum(local_groups, "wide") / NBEST
    return doc_peak - jnp.dot(member, group_mean, precision=highest)


def solution(mesh):
    placed = (
        P(("parts", "wide"), "narrow"),
        P(("parts", "wide"), "narrow"),
        P("parts"),
        P(("parts", "wide")),
        P(),
        P(),
        P(),
    )
    return jax.shard_map(
        local, mesh=mesh, in_specs=placed, out_specs=P(("parts", "wide"), "narrow"), check_vma=False
    )
```

profile of v0, /device:TPU:0, one launch (start us, length us, event | category | flops | bytes accessed | tf_op | source)
XLA Modules:
  0.0 206.9 jit_solution(12235561874789354840)
XLA Ops:
  6.5 2.4 %copy.61 = bf16[128,4096]{1,0:T(8,128)(2,1)} copy(bf16[128,4096]{1,0:T(8,128)(2,1)} %param.10) | data formatting | bytes 2097152
  8.9 1.3 copy.43
  10.3 6.4 %all-to-all-start = ((bf16[4,40,32,128]{3,2,1,0:T(8,128)(2,1)}), bf16[4,40,32,128]{3,2,1,0:T(8,128)(2,1)S(1)}, u32[]{:S(2)}, u32[]{:S(2)}) async-start(bf16[4,40,32,128]{3,2,1,0:T(8,128)(2,1)} %bitcast.20), calls=%async_computation | async-start | bytes 2621440 | tf_op jit(solution)/shard_map/all_to_all | solution.py:50
  16.8 31.2 %all-to-all-done = bf16[4,40,32,128]{3,2,1,0:T(8,128)(2,1)S(1)} async-done(((bf16[4,40,32,128]{3,2,1,0:T(8,128)(2,1)}), bf16[4,40,32,128]{3,2,1,0:T(8,128)(2,1)S(1)}, u32[]{:S(2)}, u32[]{:S(2)}) %all-to-all-start) | async-done | bytes 1310752 | tf_op jit(solution)/shard_map/all_to_all | solution.py:50
  48.1 0.3 copy.31
  48.5 1.2 fusion.8
  49.7 2.3 %fusion.5 = f32[40,128,128]{2,1,0:T(8,128)S(1)} fusion(f32[40,128,128]{1,2,0:T(8,128)S(1)} %fusion.8, f32[128,128]{1,0:T(8,128)S(1)} %copy-done.5), kind=kOutput, calls=%fused_computation.23 | convolution fusion | flops 1006632960 | bytes 5308416 | tf_op jit(solution)/shard_map/ae,nac->nec/dot_general | solution.py:54
  52.0 2.6 %fusion = f32[40,128,128]{1,2,0:T(8,128)S(1)} fusion(f32[40,128,128]{2,1,0:T(8,128)S(1)} %fusion.5, f32[128,128]{0,1:T(8,128)S(1)} %copy.33, f32[128,128]{1,0:T(8,128)S(1)} %copy-done), kind=kOutput, calls=%fused_computation.4 | convolution fusion | flops 1007288320 | bytes 5373952 | tf_op jit(solution)/shard_map/nec,bc->neb/dot_general | solution.py:56
  54.7 2.2 %fusion.1 = bf16[1,40,128,128]{2,3,1,0:T(8,128)(2,1)S(1)} fusion(f32[40,128,128]{1,2,0:T(8,128)S(1)} %fusion, f32[128,128]{1,0:T(8,128)S(1)} %copy-done.5), kind=kOutput, calls=%fused_computation.6 | convolution fusion | flops 1007288320 | bytes 3997696 | tf_op jit(solution)/shard_map/ae,neb->nab/dot_general | solution.py:57
  56.9 1.9 copy.36
  58.8 3.7 %all-to-all-start.1 = ((bf16[1,40,128,128]{3,1,0,2:T(8,128)(2,1)}), bf16[1,40,128,128]{3,1,0,2:T(8,128)(2,1)S(1)}, u32[]{:S(2)}, u32[]{:S(2)}) async-start(bf16[1,40,128,128]{3,1,0,2:T(8,128)(2,1)} %copy.36), calls=%async_computation.1 | async-start | bytes 2621440 | tf_op jit(solution)/shard_map/all_to_all | solution.py:59
  62.4 0.2 all-reduce.20.cloned.1.call-start
  62.8 0.2 slice.247
  63.1 0.2 slice.251
  63.3 0.2 slice.254
  63.5 0.2 slice.258
  65.2 0.6 slice.294
  66.5 0.2 slice.252
  66.7 0.2 slice.245
  66.9 0.7 slice.302
  67.8 25.5 %all-to-all-done.1 = bf16[1,40,128,128]{3,1,0,2:T(8,128)(2,1)S(1)} async-done(((bf16[1,40,128,128]{3,1,0,2:T(8,128)(2,1)}), bf16[1,40,128,128]{3,1,0,2:T(8,128)(2,1)S(1)}, u32[]{:S(2)}, u32[]{:S(2)}) %all-to-all-start.1) | async-done | bytes 1310752 | tf_op jit(solution)/shard_map/all_to_all | solution.py:59
  93.3 0.3 copy.37
  93.6 0.3 copy.38
  93.8 0.6 copy.47
  94.5 1.9 convolution_dynamic-update-slice_fusion.1
  96.4 47.9 %while.17 = (s32[]{:T(128)}, bf16[128,4096]{1,0:T(8,128)(2,1)}, f32[160,512]{1,0:T(8,128)S(1)}, bf16[160,4096]{1,0:T(8,128)(2,1)S(1)}, s32[]{:T(128)}, /*index=5...) while((s32[]{:T(128)}, bf16[128,4096]{1,0:T(8,128)(2,1)}, ...), condition=%wide.region_2.3_spmd, body=%wide.region_1.2_spmd.sunk | while | flops 167772176 | bytes 8732992 | solution.py:76
  96.5 14.4 %collective-permute-done = bf16[128,4096]{1,0:T(8,128)(2,1)S(1)} collective-permute-done((bf16[128,4096]{1,0:T(8,128)(2,1)}, bf16[128,4096]{1,0:T(8,128)(2,1)S(1)}, u32[]{:S(2)}, u32[]{:S(2)}) %collective-permute-start) | collective-permute-done | bytes 1048608 | tf_op jit(solution)/shard_map/while/body/eval_jaxpr/ppermute | solution.py:17
  110.9 1.0 copy.57
  111.8 0.5 convolution_dynamic-update-slice_fusion.3
  112.5 14.4 %collective-permute-done = bf16[128,4096]{1,0:T(8,128)(2,1)S(1)} collective-permute-done((bf16[128,4096]{1,0:T(8,128)(2,1)}, bf16[128,4096]{1,0:T(8,128)(2,1)S(1)}, u32[]{:S(2)}, u32[]{:S(2)}) %collective-permute-start) | collective-permute-done | bytes 1048608 | tf_op jit(solution)/shard_map/while/body/eval_jaxpr/ppermute | solution.py:17
  126.8 1.0 copy.57
  127.8 0.5 convolution_dynamic-update-slice_fusion.3
  128.4 14.4 %collective-permute-done = bf16[128,4096]{1,0:T(8,128)(2,1)S(1)} collective-permute-done((bf16[128,4096]{1,0:T(8,128)(2,1)}, bf16[128,4096]{1,0:T(8,128)(2,1)S(1)}, u32[]{:S(2)}, u32[]{:S(2)}) %collective-permute-start) | collective-permute-done | bytes 1048608 | tf_op jit(solution)/shard_map/while/body/eval_jaxpr/ppermute | solution.py:17
  142.8 1.0 copy.57
  143.8 0.5 convolution_dynamic-update-slice_fusion.3
  144.3 1.0 copy.39
  145.3 0.7 gather_fusion
  146.0 36.8 %all-reduce.20.cloned.1.call-done = f32[160,512]{0,1:T(8,128)} async-done(((f32[160,512]{0,1:T(8,128)}), f32[160,512]{0,1:T(8,128)}) %all-reduce.20.cloned.1.call-update) | async-done | bytes 327696 | tf_op jit(solution)/shard_map/psum | solution.py:79
  182.9 1.9 slice.248
  184.8 1.9 slice.249
  188.0 0.2 slice.253
  188.4 0.6 broadcast_select_fusion
  189.0 0.6 fusion.23
  190.9 0.8 copy-done.4
  191.7 0.4 slice.246
  192.4 0.6 gather_fusion.1
  193.2 6.0 %psum.15 = f32[40,16]{0,1:T(8,128)S(1)} all-reduce(f32[40,16]{0,1:T(8,128)S(1)} %fusion.3), channel_id=1, replica_groups=mesh['parts'=2,'wide'=4,'narrow'=4] {'wide'}, use_global_device_ids=true, to_apply=%region_4.5 | all-reduce | flops 640 | bytes 5120 | tf_op jit(solution)/shard_map/psum | solution.py:87
  199.2 0.9 convolution_subtract_fusion
  (131 shorter events, 5.6 us)
Async XLA Ops:
  6.5 41.9 %copy-start = (f32[128,128]{1,0:T(8,128)S(1)}, f32[128,128]{1,0:T(8,128)}, u32[]{:S(2)}) copy-start(f32[128,128]{1,0:T(8,128)} %param.15) | copy-start | bytes 196612
  6.5 2.4 %copy-start.3 = (bf16[160,4096]{1,0:T(8,128)(2,1)S(1)}, bf16[160,4096]{1,0:T(8,128)(2,1)}, u32[]{:S(2)}) copy-start(bf16[160,4096]{1,0:T(8,128)(2,1)} %param.9) | copy-start | bytes 3932164
  10.3 6.5 %copy-start.6 = (f32[128,128]{1,0:T(8,128)S(1)}, f32[128,128]{1,0:T(8,128)}, u32[]{:S(2)}) copy-start(f32[128,128]{1,0:T(8,128)} %param.13) | copy-start | bytes 196612
  10.3 37.8 %all-to-all-start = ((bf16[4,40,32,128]{3,2,1,0:T(8,128)(2,1)}), bf16[4,40,32,128]{3,2,1,0:T(8,128)(2,1)S(1)}, u32[]{:S(2)}, u32[]{:S(2)}) async-start(bf16[4,40,32,128]{3,2,1,0:T(8,128)(2,1)} %bitcast.20), calls=%async_computation | async-start | bytes 2621440 | tf_op jit(solution)/shard_map/all_to_all | solution.py:50
  48.4 1.3 copy-start.5
  58.8 3.9 %copy-start.1 = (s32[512]{0:T(512)S(1)}, s32[512]{0:T(512)}, u32[]{:S(2)}) copy-start(s32[512]{0:T(512)} %param.11) | copy-start | bytes 6148
  58.8 34.5 %all-to-all-start.1 = ((bf16[1,40,128,128]{3,1,0,2:T(8,128)(2,1)}), bf16[1,40,128,128]{3,1,0,2:T(8,128)(2,1)S(1)}, u32[]{:S(2)}, u32[]{:S(2)}) async-start(bf16[1,40,128,128]{3,1,0,2:T(8,128)(2,1)} %copy.36), calls=%async_computation.1 | async-start | bytes 2621440 | tf_op jit(solution)/shard_map/all_to_all | solution.py:59
  62.4 120.4 %all-reduce.20.cloned.1.call-start = ((), (), s32[]{:S(2)}) async-start(), calls=%async_computation.2 | async-start | bytes 1048576 | tf_op jit(solution)/shard_map/psum | solution.py:79
  96.4 14.5 %collective-permute-start = (bf16[128,4096]{1,0:T(8,128)(2,1)}, bf16[128,4096]{1,0:T(8,128)(2,1)S(1)}, u32[]{:S(2)}, u32[]{:S(2)}) collective-permute-start(bf16[128,4096]{1,0:T(8,128)(2,1)} %get-tuple-element.198), channel_id=1, source_target_pairs={{0,4},{4,8},{8,12},{12,0},{1,5},{5,9},{9,13},{13,1},{2,6},{6,10},{... | collective-permute-start | bytes 3145736 | tf_op jit(solution)/shard_map/while/body/eval_jaxpr/ppermute | solution.py:17
  112.4 14.5 %collective-permute-start = (bf16[128,4096]{1,0:T(8,128)(2,1)}, bf16[128,4096]{1,0:T(8,128)(2,1)S(1)}, u32[]{:S(2)}, u32[]{:S(2)}) collective-permute-start(bf16[128,4096]{1,0:T(8,128)(2,1)} %get-tuple-element.198), channel_id=1, source_target_pairs={{0,4},{4,8},{8,12},{12,0},{1,5},{5,9},{9,13},{13,1},{2,6},{6,10},{... | collective-permute-start | bytes 3145736 | tf_op jit(solution)/shard_map/while/body/eval_jaxpr/ppermute | solution.py:17
  128.3 14.5 %collective-permute-start = (bf16[128,4096]{1,0:T(8,128)(2,1)}, bf16[128,4096]{1,0:T(8,128)(2,1)S(1)}, u32[]{:S(2)}, u32[]{:S(2)}) collective-permute-start(bf16[128,4096]{1,0:T(8,128)(2,1)} %get-tuple-element.198), channel_id=1, source_target_pairs={{0,4},{4,8},{8,12},{12,0},{1,5},{5,9},{9,13},{13,1},{2,6},{6,10},{... | collective-permute-start | bytes 3145736 | tf_op jit(solution)/shard_map/while/body/eval_jaxpr/ppermute | solution.py:17
  186.8 3.1 %copy-start.2 = (f32[160,256]{0,1:T(8,128)}, f32[160,256]{0,1:T(8,128)S(1)}, u32[]{:S(2)}) copy-start(f32[160,256]{0,1:T(8,128)S(1)} %maximum_select_fusion.1) | copy-start | bytes 491524
  190.0 0.7 slice-start
  190.7 1.0 copy-start.4
  190.8 1.4 slice-start.1
  192.3 0.7 copy-start.7
Sparse Core Ops, SparseCore 0:
  145.4 37.3 all-reduce.19
where the time goes:
time: 208 us; the launch traced here: 207 us
  waiting for transfers between devices  137 us (66%)
  local copies, waits for them, and re-layouts  23.4 us (11%)
  between operations  14 us (7%)
  matrix products  12.9 us (6%)
  starting transfers between devices  10.5 us (5%)
  blocking collectives  5.99 us (3%)
  other arithmetic  3.23 us (2%)
    ppermute x3, waiting for transfers between devices, shifted(): return lax.ppermute(value, axis, pairs)  43.2 us
    psum x1, waiting for transfers between devices, local(): summed = lax.psum(score_tile, 'narrow')  36.8 us
    all_to_all x1, waiting for transfers between devices, local(): lax.all_to_all(gradient_pieces, 'narrow', split_axis=0, concat_axis=2, ti...  31.2 us
    all_to_all x1, waiting for transfers between devices, local(): lax.all_to_all(rounded, 'narrow', split_axis=2, concat_axis=0, tiled=True)  25.5 us
    slice x57, local copies, waits for them, and re-layouts, segment_peaks(): lax.associative_scan(keep_peak, (score_rows, starts_wide), axis=1)  9.89 us
    all_to_all x1, starting transfers between devices, local(): lax.all_to_all(gradient_pieces, 'narrow', split_axis=0, concat_axis=2, ti...  6.45 us
    psum x1, blocking collectives, local(): group_mean = lax.psum(local_groups, 'wide') / NBEST  5.99 us
    unnamed x19, local copies, waits for them, and re-layouts  5.17 us
  transfers between devices with their start and end apart: 6, of which 6 were waited for; matrix products, arithmetic and copies ran while one was open for 3% of the time, Pallas kernels for 0%

commit v1 on v0

v1 whole, which is shorter than its diff:
```python
import functools

import jax
import jax.numpy as jnp
from jax import lax
from jax.experimental import pallas as pl
from jax.experimental.pallas import tpu as pltpu
from jax.sharding import PartitionSpec as P

DOCS_DEV = 16
NBEST = 16
SPAN_MOST = 32
CORES = 2
DAMPING = 0.05
LOWEST = -1e30

MESH = pl.DeviceIdType.MESH
HIGHEST = lax.Precision.HIGHEST
ROW_BY_ROW = (((1,), (1,)), ((), ()))


def split(value):
    high = value.astype(jnp.bfloat16)
    return high, (value - high.astype(jnp.float32)).astype(jnp.bfloat16)


def product(left, right):
    return jnp.dot(left, right, preferred_element_type=jnp.float32)


def stack_rows(pieces):
    if pieces[0].shape[0] % 16:
        joined = jnp.concatenate([piece.astype(jnp.float32) for piece in pieces], axis=0)
        return joined.astype(jnp.bfloat16)
    return jnp.concatenate(pieces, axis=0)


def kernel(
    chunks, t_ref, g_ref, span_ref, group_ref, eig_ref, in_ref, basis_ref, out_ref,
    taken, made, held, gathered, scores, shares, peaks_out, peaks_in, sums,
    t_send, t_recv, m_send, m_recv, g_send, g_pass, g_recv, s_send, s_recv,
    p_send, p_recv, q_send, q_recv, t_local, g_local,
):
    wide, narrow = lax.axis_size("wide"), lax.axis_size("narrow")
    w, z = lax.axis_index("wide"), lax.axis_index("narrow")
    chips = wide // CORES
    chip, core = w // CORES, lax.rem(w, CORES)
    sibling = chip * CORES + 1 - core
    rows = taken.shape[2]
    local_in = taken.shape[3] // 128
    size = basis_ref.shape[0]

    def other(index, step, count):
        return lax.rem(index + step, count)

    def remote(source, target, send, recv, device):
        return pltpu.make_async_remote_copy(
            src_ref=source, dst_ref=target, send_sem=send, recv_sem=recv,
            device_id=device, device_id_type=MESH,
        )

    def rows_copy(chunk, peer, slot):
        return remote(
            t_ref.at[chunk, peer], taken.at[chunk, slot],
            t_send.at[chunk, peer], t_recv.at[chunk, slot], {"narrow": peer},
        )

    def made_copy(chunk, peer, slot):
        return remote(
            made.at[chunk, peer], held.at[chunk, slot],
            m_send.at[chunk, peer], m_recv.at[chunk, slot], {"narrow": peer},
        )

    def grad_copy(there, slot):
        return remote(
            g_ref, gathered.at[slot], g_send.at[there], g_recv.at[slot],
            {"wide": there * CORES + core},
        )

    def pass_copy(here, slot):
        return remote(
            gathered.at[slot], gathered.at[slot], g_pass.at[here], g_recv.at[slot], {"wide": sibling}
        )

    def own_pass(slot):
        return remote(g_ref, gathered.at[slot], g_pass.at[chip], g_recv.at[slot], {"wide": sibling})

    def share_copy(peer, slot):
        return remote(
            scores.at[peer], shares.at[slot], s_send.at[peer], s_recv.at[slot], {"narrow": peer}
        )

    def peak_copy(docs, slot):
        return remote(
            peaks_out.at[docs], peaks_in.at[slot], p_send.at[docs], p_recv.at[slot],
            {"wide": z, "narrow": docs},
        )

    def sum_copy(peer, slot):
        return remote(sums.at[w], sums.at[slot], q_send.at[peer], q_recv.at[slot], {"wide": peer})

    barrier = pltpu.get_barrier_semaphore()
    for step in range(1, narrow):
        pl.semaphore_signal(
            barrier, inc=1, device_id={"narrow": other(z, step, narrow)}, device_id_type=MESH
        )
    for step in range(1, wide):
        peer = other(w, step, wide)
        pl.semaphore_signal(barrier, inc=1, device_id={"wide": peer}, device_id_type=MESH)
        pl.semaphore_signal(
            barrier, inc=1, device_id={"wide": peer, "narrow": w}, device_id_type=MESH
        )
    pl.semaphore_wait(barrier, narrow - 1 + wide - 1 + jnp.where(w == z, 0, narrow))

    own_rows = [
        pltpu.make_async_copy(t_ref.at[chunk, z], taken.at[chunk, z], t_local.at[chunk])
        for chunk in range(chunks)
    ]
    own_grads = pltpu.make_async_copy(g_ref, gathered.at[w], g_local)
    for chunk in range(chunks):
        for step in range(1, narrow):
            rows_copy(chunk, other(z, step, narrow), z).start()
        own_rows[chunk].start()
        if chunk == 0:
            for step in range(1, chips):
                grad_copy(other(chip, step, chips), w).start()
            own_pass(w).start()
            own_grads.start()

    in_basis, out_basis = in_ref[...], basis_ref[...]
    in_high, in_low = split(in_basis)
    inT_high, inT_low = split(in_basis.T)
    out_high, out_low = split(out_basis)
    outT_high, outT_low = split(out_basis.T)
    into = jnp.concatenate([out_high, out_low], axis=1)
    back = jnp.concatenate(
        [
            jnp.concatenate([outT_high, outT_low], axis=1),
            jnp.concatenate([outT_high, jnp.zeros_like(outT_low)], axis=1),
        ],
        axis=0,
    )
    in_into = jnp.concatenate([inT_high, inT_high, inT_low], axis=1)
    in_back = jnp.concatenate([in_high, in_high, in_low], axis=1)
    weight = 1.0 / (eig_ref[...] + DAMPING)

    def mixed(matrix, blocks):
        wide_block = jnp.concatenate(blocks, axis=1)
        high, low = split(wide_block)
        return product(matrix, jnp.concatenate([high, low, high], axis=0))

    def lane_block(value, index):
        return value[:, index * size : (index + 1) * size]

    def precondition(chunk):
        pieces = [
            taken[chunk, source, :, a * size : (a + 1) * size]
            for source in range(narrow)
            for a in range(local_in)
        ]
        both = product(stack_rows(pieces), into)
        left = both[:, :size] + both[:, size:]
        left = jnp.swapaxes(left.reshape(size, rows, size), 0, 1)
        rotated = mixed(in_into, [left[row] for row in range(rows)])
        scaled = jnp.concatenate([lane_block(rotated, row) * weight for row in range(rows)], axis=0)
        both = product(jnp.concatenate(split(scaled), axis=1), back)
        right = both[:, :size] + both[:, size:]
        restored = mixed(in_back, [right[row * size : (row + 1) * size] for row in range(rows)])
        result = jnp.stack([lane_block(restored, row) for row in range(rows)], axis=0)
        result = jnp.swapaxes(result, 0, 1).astype(jnp.bfloat16)
        for target in range(narrow):
            for a in range(local_in):
                made[chunk, target, :, a * size : (a + 1) * size] = result[target * local_in + a]

    for chunk in range(chunks):
        own_rows[chunk].wait()
        for step in range(1, narrow):
            rows_copy(chunk, z, other(z, step, narrow)).wait_recv()
        precondition(chunk)
        for step in range(1, narrow):
            made_copy(chunk, other(z, step, narrow), z).start()
        held[chunk, z] = made[chunk, z]

    for step in range(1, chips):
        there = other(chip, step, chips)
        slot = there * CORES + core
        grad_copy(there, slot).wait_recv()
        pass_copy(there, slot).start()
    own_grads.wait()
    for step in range(chips):
        there = other(chip, step, chips)
        pass_copy(there, there * CORES + 1 - core).wait_recv()

    for chunk in range(chunks):
        for step in range(1, narrow):
            made_copy(chunk, z, other(z, step, narrow)).wait_recv()
        width = narrow * rows

        def score(block, unused, chunk=chunk, width=width):
            train = stack_rows([held[chunk, source] for source in range(narrow)])
            scores[block, :, chunk * width : (chunk + 1) * width] = lax.dot_general(
                gathered[block], train, ROW_BY_ROW, preferred_element_type=jnp.float32
            )
            return unused

        lax.fori_loop(0, wide, score, 0)

    for step in range(1, narrow):
        share_copy(other(z, step, narrow), z).start()
    span = jnp.broadcast_to(span_ref[pl.ds(w, 1), :], (8, span_ref.shape[1]))
    lane = lax.broadcasted_iota(jnp.int32, span.shape, 1)
    row_count = span.shape[1]
    total = scores[z]
    for step in range(1, narrow):
        source = other(z, step, narrow)
        share_copy(z, source).wait_recv()
        total = total + shares[source]

    distance = 1
    while distance < min(SPAN_MOST, row_count):
        same = (pltpu.roll(span, distance, 1) == span) & (lane >= distance)
        earlier = jnp.where(same[:1], pltpu.roll(total, distance, 1), total)
        total = jnp.maximum(total, earlier)
        distance *= 2
    last = (pltpu.roll(span, row_count - 1, 1) != span) | (lane == row_count - 1)
    doc_share = peaks_out.shape[1]
    docs = doc_share * narrow
    wanted = lax.broadcasted_iota(jnp.int32, (docs, row_count), 0)
    pick = ((span[:1] == wanted) & last[:1]).astype(jnp.float32)
    peaks = lax.dot_general(
        pick, total, ROW_BY_ROW, precision=HIGHEST, preferred_element_type=jnp.float32
    )
    peaks = jnp.where(jnp.sum(pick, axis=1, keepdims=True) > 0, peaks, LOWEST)
    for index in range(narrow):
        peaks_out[index] = peaks[index * doc_share : (index + 1) * doc_share]
    for step in range(1, narrow):
        peak_copy(other(z, step, narrow), w).start()

    @pl.when(w != z)
    def _():
        peak_copy(z, w).start()

    @pl.when(w == z)
    def _():
        peaks_in[w] = peaks_out[z]

    group_slots = sums.shape[2]
    cands = group_ref.shape[1]
    member = (
        group_ref[...] == lax.broadcasted_iota(jnp.int32, (group_slots, cands), 0)
    ).astype(jnp.float32)
    for step in range(1, wide):
        peak_copy(z, other(w, step, wide)).wait_recv()

    @pl.when(w != z)
    def _():
        peak_copy(z, w).wait_recv()

    doc_peak = peaks_in[0]
    for index in range(1, wide):
        doc_peak = jnp.maximum(doc_peak, peaks_in[index])
    sums[w] = lax.dot_general(
        doc_peak, member, ROW_BY_ROW, precision=HIGHEST, preferred_element_type=jnp.float32
    )
    for step in range(1, wide):
        sum_copy(other(w, step, wide), w).start()
    for step in range(1, wide):
        sum_copy(w, other(w, step, wide)).wait_recv()
    mean = sums[0]
    for index in range(1, wide):
        mean = mean + sums[index]
    out_ref[...] = doc_peak - jnp.dot(
        mean * (1.0 / NBEST), member, precision=HIGHEST, preferred_element_type=jnp.float32
    )

    for chunk in range(chunks):
        for step in range(1, narrow):
            rows_copy(chunk, other(z, step, narrow), z).wait_send()
            made_copy(chunk, other(z, step, narrow), z).wait_send()
    for step in range(1, chips):
        there = other(chip, step, chips)
        grad_copy(there, w).wait_send()
        pass_copy(there, there * CORES + core).wait_send()
    own_pass(w).wait_send()
    for step in range(1, narrow):
        share_copy(other(z, step, narrow), z).wait_send()
        peak_copy(other(z, step, narrow), w).wait_send()

    @pl.when(w != z)
    def _():
        peak_copy(z, w).wait_send()

    for step in range(1, wide):
        sum_copy(other(w, step, wide), w).wait_send()


def solution(mesh):
    wide, narrow = mesh.shape["wide"], mesh.shape["narrow"]
    assert wide == narrow

    def local(cand_grads, train_feats, span_ids, group_ids, eig_values, input_basis, basis):
        cands, width = cand_grads.shape
        train_rows = train_feats.shape[0]
        peer_rows = train_rows // narrow
        chunks = max(1, peer_rows // 16)
        rows = peer_rows // chunks
        doc_share = DOCS_DEV * wide // narrow
        group_slots = -(-(cands * wide // NBEST) // 128) * 128
        in_vmem = pl.BlockSpec(memory_space=pltpu.VMEM)
        anywhere = pl.BlockSpec(memory_space=pl.ANY)
        dma = pltpu.SemaphoreType.DMA
        turned = pl.pallas_call(
            functools.partial(kernel, chunks),
            out_shape=jax.ShapeDtypeStruct((doc_share, cands), jnp.float32),
            in_specs=[anywhere, anywhere] + [in_vmem] * 5,
            out_specs=in_vmem,
            scratch_shapes=[
                pltpu.VMEM((chunks, narrow, rows, width), jnp.bfloat16),
                pltpu.VMEM((chunks, narrow, rows, width), jnp.bfloat16),
                pltpu.VMEM((chunks, narrow, rows, width), jnp.bfloat16),
                pltpu.VMEM((wide, cands, width), jnp.bfloat16),
                pltpu.VMEM((wide, cands, train_rows), jnp.float32),
                pltpu.VMEM((narrow, cands, train_rows), jnp.float32),
                pltpu.VMEM((narrow, doc_share, cands), jnp.float32),
                pltpu.VMEM((wide, doc_share, cands), jnp.float32),
                pltpu.VMEM((wide, doc_share, group_slots), jnp.float32),
                dma((chunks, narrow)),
                dma((chunks, narrow)),
                dma((chunks, narrow)),
                dma((chunks, narrow)),
                dma((wide // CORES,)),
                dma((wide // CORES,)),
                dma((wide,)),
                dma((narrow,)),
                dma((narrow,)),
                dma((narrow,)),
                dma((wide,)),
                dma((wide,)),
                dma((wide,)),
                dma((chunks,)),
                dma(()),
            ],
            compiler_params=pltpu.CompilerParams(
                collective_id=0, has_side_effects=True, vmem_limit_bytes=48 * 2**20
            ),
        )(
            train_feats.reshape(chunks, narrow, rows, width),
            cand_grads,
            span_ids.reshape(wide, train_rows),
            group_ids.reshape(1, cands),
            eig_values,
            input_basis,
            basis,
        )
        return turned.T

    return jax.shard_map(
        local,
        mesh=mesh,
        in_specs=(
            P(("parts", "wide"), "narrow"),
            P(("parts", "wide"), "narrow"),
            P("parts"),
            P(("parts", "wide")),
            P(),
            P(),
            P(),
        ),
        out_specs=P(("parts", "wide"), "narrow"),
        check_vma=False,
    )
```

time: 208 us -> 79.6 us (0.38)
  waiting for transfers between devices: 137 us -> 0 us
  Pallas kernels: 0 us -> 72.2 us
  local copies, waits for them, and re-layouts: 23.4 us -> 7.02 us
  between operations: 14 us -> 0.02 us
  matrix products: 12.9 us -> 0 us
  starting transfers between devices: 10.5 us -> 0 us
  blocking collectives: 5.99 us -> 0 us
  other arithmetic: 3.23 us -> 0 us
    pallas_call x0 -> x1, Pallas kernels: none -> 72.2 us  [local(): pl.pallas_call(functools.partial(kernel, chunks), out_shape=jax.ShapeDtyp...]
    all_to_all x2 -> x0, waiting for transfers between devices: 56.7 us -> none  [the longest x1 31.2 us: local(): lax.all_to_all(gradient_pieces, 'narrow', split_axis=0, concat_axis=2, ti...]
    ppermute x3 -> x0, waiting for transfers between devices: 43.2 us -> none  [shifted(): return lax.ppermute(value, axis, pairs)]
    psum x1 -> x0, waiting for transfers between devices: 36.8 us -> none  [local(): summed = lax.psum(score_tile, 'narrow')]
    dot_general x10 -> x0, matrix products: 12.9 us -> none  [the longest x4 3.41 us: add_block(): lax.dot_general(precond, train_block, (((1,), (1,)), ((), ())), preferred...]
    all_to_all x2 -> x0, starting transfers between devices: 10.1 us -> none  [the longest x1 6.45 us: local(): lax.all_to_all(gradient_pieces, 'narrow', split_axis=0, concat_axis=2, ti...]
    slice x57 -> x0, local copies, waits for them, and re-layouts: 9.89 us -> none  [segment_peaks(): lax.associative_scan(keep_peak, (score_rows, starts_wide), axis=1)]
    psum x1 -> x0, blocking collectives: 5.99 us -> none  [local(): group_mean = lax.psum(local_groups, 'wide') / NBEST]
  transfers between devices with their start and end apart: 6 -> 0, of which waited for: 6 -> 0; matrix products, arithmetic and copies ran while one was open for 3% -> 0% of each run, Pallas kernels for 0% -> 0%
where the time goes in v1:
time: 79.6 us; the launch traced here: 79.2 us
  Pallas kernels  72.2 us (91%)
  local copies, waits for them, and re-layouts  7.02 us (9%)
    pallas_call x1, Pallas kernels, local(): pl.pallas_call(functools.partial(kernel, chunks), out_shape=jax.ShapeDtyp...  72.2 us
    unnamed x15, local copies, waits for them, and re-layouts  7.02 us

profile of v1, /device:TPU:0, one launch (start us, length us, event | category | flops | bytes accessed | tf_op | source)
XLA Modules:
  0.0 79.2 jit_solution(15076032272497385282)
XLA Ops:
  0.0 0.0 copy-start
  0.0 1.3 %copy-done = bf16[160,4096]{1,0:T(8,128)(2,1)S(1)} copy-done((bf16[160,4096]{1,0:T(8,128)(2,1)S(1)}, bf16[160,4096]{1,0:T(8,128)(2,1)}, u32[]{:S(2)}) %copy-start) | copy-done | bytes 1310744
  1.3 0.0 copy-start.1
  1.3 1.2 %copy-done.1 = bf16[128,4096]{1,0:T(8,128)(2,1)S(1)} copy-done((bf16[128,4096]{1,0:T(8,128)(2,1)S(1)}, bf16[128,4096]{1,0:T(8,128)(2,1)}, u32[]{:S(2)}) %copy-start.1) | copy-done | bytes 1048600
  2.5 0.0 copy-start.2
  2.5 0.8 %copy-done.2 = f32[128,128]{1,0:T(8,128)S(1)} copy-done((f32[128,128]{1,0:T(8,128)S(1)}, f32[128,128]{1,0:T(8,128)}, u32[]{:S(2)}) %copy-start.2) | copy-done | bytes 65560
  3.4 0.0 copy-start.3
  3.4 0.8 %copy-done.3 = f32[128,128]{1,0:T(8,128)S(1)} copy-done((f32[128,128]{1,0:T(8,128)S(1)}, f32[128,128]{1,0:T(8,128)}, u32[]{:S(2)}) %copy-start.3) | copy-done | bytes 65560
  4.2 0.0 copy-start.4
  4.2 0.8 %copy-done.4 = f32[128,128]{1,0:T(8,128)S(1)} copy-done((f32[128,128]{1,0:T(8,128)S(1)}, f32[128,128]{1,0:T(8,128)}, u32[]{:S(2)}) %copy-start.4) | copy-done | bytes 65560
  5.1 0.0 copy-start.5
  5.1 0.7 copy-done.5
  5.7 0.0 copy-start.6
  5.7 0.7 copy-done.6
  6.4 72.2 %shard_map.73 = f32[16,160]{1,0:T(8,128)S(1)} custom-call(bf16[2,4,16,4096]{3,2,1,0:T(8,128)(2,1)S(1)} %bitcast.4, bf16[160,4096]{1,0:T(8,128)(2,1)S(1)} %copy-done, s32[4,128]{1,0:T(4,128)S(1)} %bitcast.6, s32[1,160]{1,0:T(1,128)S(1)} %bitcast.7, f32[128,128]{1,0:T(8,128)S(1)} %copy-done.2, f32[128,128]{1,0:T(8,128)S(1)} %copy-done.3, f32[128,128]{1,0:T(8,128)S(1)} %copy-done.4), custom_call_target="tpu_custom_call" | custom-call | tf_op jit(solution)/shard_map/pallas_call | solution.py:312
  78.6 0.6 copy.9
Async XLA Ops:
  0.0 1.3 %copy-start = (bf16[160,4096]{1,0:T(8,128)(2,1)S(1)}, bf16[160,4096]{1,0:T(8,128)(2,1)}, u32[]{:S(2)}) copy-start(bf16[160,4096]{1,0:T(8,128)(2,1)} %g_ref.1) | copy-start | bytes 3932164
  1.3 1.2 %copy-start.1 = (bf16[128,4096]{1,0:T(8,128)(2,1)S(1)}, bf16[128,4096]{1,0:T(8,128)(2,1)}, u32[]{:S(2)}) copy-start(bf16[128,4096]{1,0:T(8,128)(2,1)} %param.8) | copy-start | bytes 3145732
  2.5 0.8 %copy-start.2 = (f32[128,128]{1,0:T(8,128)S(1)}, f32[128,128]{1,0:T(8,128)}, u32[]{:S(2)}) copy-start(f32[128,128]{1,0:T(8,128)} %eig_ref.1) | copy-start | bytes 196612
  3.4 0.8 %copy-start.3 = (f32[128,128]{1,0:T(8,128)S(1)}, f32[128,128]{1,0:T(8,128)}, u32[]{:S(2)}) copy-start(f32[128,128]{1,0:T(8,128)} %in_ref.1) | copy-start | bytes 196612
  4.2 0.8 %copy-start.4 = (f32[128,128]{1,0:T(8,128)S(1)}, f32[128,128]{1,0:T(8,128)}, u32[]{:S(2)}) copy-start(f32[128,128]{1,0:T(8,128)} %basis_ref.1) | copy-start | bytes 196612
  5.1 0.7 copy-start.5
  5.7 0.7 copy-start.6

commit v2 on v1

--- a/solution.py
+++ b/solution.py
@@ -36,10 +36,10 @@
 
 
 def kernel(
-    chunks, t_ref, g_ref, span_ref, group_ref, eig_ref, in_ref, basis_ref, out_ref,
-    taken, made, held, gathered, scores, shares, peaks_out, peaks_in, sums,
+    chunks, t_ref, g_ref, span_hbm, group_hbm, eig_hbm, in_hbm, basis_hbm, out_ref,
+    span_ref, group_ref, eig_ref, in_ref, basis_ref, taken, made, held, gathered, scores, shares, peaks_out, peaks_in, sums,
     t_send, t_recv, m_send, m_recv, g_send, g_pass, g_recv, s_send, s_recv,
-    p_send, p_recv, q_send, q_recv, t_local, g_local,
+    p_send, p_recv, q_send, q_recv, t_local, g_local, small,
 ):
     wide, narrow = lax.axis_size("wide"), lax.axis_size("narrow")
     w, z = lax.axis_index("wide"), lax.axis_index("narrow")
@@ -99,6 +99,20 @@
     def sum_copy(peer, slot):
         return remote(sums.at[w], sums.at[slot], q_send.at[peer], q_recv.at[slot], {"wide": peer})
 
+    fetches = [
+        pltpu.make_async_copy(source, target, small.at[index])
+        for index, (source, target) in enumerate(
+            (
+                (in_hbm, in_ref),
+                (basis_hbm, basis_ref),
+                (eig_hbm, eig_ref),
+                (span_hbm, span_ref),
+                (group_hbm, group_ref),
+            )
+        )
+    ]
+    for fetch in fetches:
+        fetch.start()
     barrier = pltpu.get_barrier_semaphore()
     for step in range(1, narrow):
         pl.semaphore_signal(
@@ -127,6 +141,8 @@
             own_pass(w).start()
             own_grads.start()
 
+    for fetch in fetches:
+        fetch.wait()
     in_basis, out_basis = in_ref[...], basis_ref[...]
     in_high, in_low = split(in_basis)
     inT_high, inT_low = split(in_basis.T)
@@ -307,14 +323,19 @@
         doc_share = DOCS_DEV * wide // narrow
         group_slots = -(-(cands * wide // NBEST) // 128) * 128
         in_vmem = pl.BlockSpec(memory_space=pltpu.VMEM)
-        anywhere = pl.BlockSpec(memory_space=pl.ANY)
+        anywhere = pl.BlockSpec(memory_space=pltpu.HBM)
         dma = pltpu.SemaphoreType.DMA
         turned = pl.pallas_call(
             functools.partial(kernel, chunks),
             out_shape=jax.ShapeDtypeStruct((doc_share, cands), jnp.float32),
-            in_specs=[anywhere, anywhere] + [in_vmem] * 5,
+            in_specs=[anywhere] * 7,
             out_specs=in_vmem,
             scratch_shapes=[
+                pltpu.VMEM((wide, train_rows), jnp.int32),
+                pltpu.VMEM((1, cands), jnp.int32),
+                pltpu.VMEM(eig_values.shape, jnp.float32),
+                pltpu.VMEM(input_basis.shape, jnp.float32),
+                pltpu.VMEM(basis.shape, jnp.float32),
                 pltpu.VMEM((chunks, narrow, rows, width), jnp.bfloat16),
                 pltpu.VMEM((chunks, narrow, rows, width), jnp.bfloat16),
                 pltpu.VMEM((chunks, narrow, rows, width), jnp.bfloat16),
@@ -339,9 +360,10 @@
                 dma((wide,)),
                 dma((chunks,)),
                 dma(()),
+                dma((5,)),
             ],
             compiler_params=pltpu.CompilerParams(
-                collective_id=0, has_side_effects=True, vmem_limit_bytes=48 * 2**20
+                collective_id=0, has_side_effects=True, vmem_limit_bytes=63 * 2**20
             ),
         )(
             train_feats.reshape(chunks, narrow, rows, width),

time: 79.6 us -> 74.6 us (0.937)
  local copies, waits for them, and re-layouts: 7.02 us -> 1.32 us
  Pallas kernels: 72.2 us -> 73 us
    unnamed x15 -> x1, local copies, waits for them, and re-layouts: 7.02 us -> 1.32 us
    pallas_call x1, Pallas kernels: 72.2 us -> 73 us  [local(): pl.pallas_call(functools.partial(kernel, chunks), out_shape=jax.ShapeDtyp...]
where the time goes in v2:
time: 74.6 us; the launch traced here: 74.4 us
  Pallas kernels  73 us (98%)
  local copies, waits for them, and re-layouts  1.32 us (2%)
    pallas_call x1, Pallas kernels, local(): pl.pallas_call(functools.partial(kernel, chunks), out_shape=jax.ShapeDtyp...  73 us

profile of v2, /device:TPU:0, one launch (start us, length us, event | category | flops | bytes accessed | tf_op | source)
XLA Modules:
  0.0 74.4 jit_solution(1316187490937539073)
XLA Ops:
  0.0 73.0 %shard_map.73 = f32[16,160]{1,0:T(8,128)} custom-call(bf16[2,4,16,4096]{3,2,1,0:T(8,128)(2,1)} %bitcast.4, bf16[160,4096]{1,0:T(8,128)(2,1)} %g_ref.1, s32[4,128]{1,0:T(4,128)} %bitcast.6, s32[1,160]{1,0:T(1,128)} %bitcast.7, f32[128,128]{1,0:T(8,128)} %eig_hbm.1, f32[128,128]{1,0:T(8,128)} %in_hbm.1, f32[128,128]{1,0:T(8,128)} %basis_hbm.1), custom_call_target="tpu_custom_call" | custom-call | tf_op jit(solution)/shard_map/pallas_call | solution.py:328
  73.0 1.3 %copy.9 = f32[160,16]{0,1:T(8,128)} copy(f32[160,16]{0,1:T(8,128)} %bitcast.5) | data formatting | bytes 20480

commit v3 on v2

--- a/solution.py
+++ b/solution.py
@@ -37,8 +37,8 @@
 
 def kernel(
     chunks, t_ref, g_ref, span_hbm, group_hbm, eig_hbm, in_hbm, basis_hbm, out_ref,
-    span_ref, group_ref, eig_ref, in_ref, basis_ref, taken, made, held, gathered, scores, shares, peaks_out, peaks_in, sums,
-    t_send, t_recv, m_send, m_recv, g_send, g_pass, g_recv, s_send, s_recv,
+    span_ref, group_ref, eig_ref, in_ref, basis_ref, taken, made, held, gathered, scores, shares, low, coarse, coarse_in, peaks_out, peaks_in, sums,
+    t_send, t_recv, m_send, m_recv, g_send, g_pass, g_recv, s_send, s_recv, c_send, c_recv,
     p_send, p_recv, q_send, q_recv, t_local, g_local, small,
 ):
     wide, narrow = lax.axis_size("wide"), lax.axis_size("narrow")
@@ -49,6 +49,8 @@
     rows = taken.shape[2]
     local_in = taken.shape[3] // 128
     size = basis_ref.shape[0]
+    pieces_out = m_send.shape[1]
+    piece_width = taken.shape[3] // pieces_out
 
     def other(index, step, count):
         return lax.rem(index + step, count)
@@ -65,10 +67,11 @@
             t_send.at[chunk, peer], t_recv.at[chunk, slot], {"narrow": peer},
         )
 
-    def made_copy(chunk, peer, slot):
-        return remote(
-            made.at[chunk, peer], held.at[chunk, slot],
-            m_send.at[chunk, peer], m_recv.at[chunk, slot], {"narrow": peer},
+    def made_copy(chunk, piece, peer, slot):
+        columns = pl.ds(piece * piece_width, piece_width)
+        return remote(
+            made.at[chunk, peer, :, columns], held.at[chunk, slot, :, columns],
+            m_send.at[chunk, piece, peer], m_recv.at[chunk, piece, slot], {"narrow": peer},
         )
 
     def grad_copy(there, slot):
@@ -88,6 +91,22 @@
     def share_copy(peer, slot):
         return remote(
             scores.at[peer], shares.at[slot], s_send.at[peer], s_recv.at[slot], {"narrow": peer}
+        )
+
+    half = narrow // 2
+    near_base = z // half * half
+    far_base = half - near_base
+
+    def near(step):
+        return near_base + lax.rem(z + step, half)
+
+    def far(step):
+        return far_base + lax.rem(z + step, half)
+
+    def coarse_copy(step, slot):
+        return remote(
+            coarse.at[step], coarse_in.at[slot], c_send.at[step], c_recv.at[slot],
+            {"narrow": far(step)},
         )
 
     def peak_copy(docs, slot):
@@ -183,18 +202,26 @@
         right = both[:, :size] + both[:, size:]
         restored = mixed(in_back, [right[row * size : (row + 1) * size] for row in range(rows)])
         result = jnp.stack([lane_block(restored, row) for row in range(rows)], axis=0)
-        result = jnp.swapaxes(result, 0, 1).astype(jnp.bfloat16)
+        exact = jnp.swapaxes(result, 0, 1)
+        result = exact.astype(jnp.bfloat16)
+        rest = exact - result.astype(jnp.float32)
         for target in range(narrow):
             for a in range(local_in):
                 made[chunk, target, :, a * size : (a + 1) * size] = result[target * local_in + a]
+            keep = jnp.where(z == target, 1.0, 0.0)
+            for a in range(local_in):
+                low[chunk, target, :, a * size : (a + 1) * size] = (
+                    rest[target * local_in + a] * keep
+                ).astype(jnp.bfloat16)
 
     for chunk in range(chunks):
         own_rows[chunk].wait()
         for step in range(1, narrow):
             rows_copy(chunk, z, other(z, step, narrow)).wait_recv()
         precondition(chunk)
-        for step in range(1, narrow):
-            made_copy(chunk, other(z, step, narrow), z).start()
+        for piece in range(pieces_out):
+            for step in range(1, narrow):
+                made_copy(chunk, piece, other(z, step, narrow), z).start()
         held[chunk, z] = made[chunk, z]
 
     for step in range(1, chips):
@@ -207,30 +234,53 @@
         there = other(chip, step, chips)
         pass_copy(there, there * CORES + 1 - core).wait_recv()
 
+    def score(chunk, piece, block):
+        width = narrow * rows
+        place = (block, slice(None), slice(chunk * width, (chunk + 1) * width))
+        columns = slice(piece * piece_width, (piece + 1) * piece_width)
+        train = stack_rows(
+            [part[chunk, source, :, columns] for part in (held, low) for source in range(narrow)]
+        )
+        value = lax.dot_general(
+            gathered[block, :, columns], train, ROW_BY_ROW, preferred_element_type=jnp.float32
+        )
+        value = value[:, :width] + value[:, width:]
+        scores[place] = value if piece == 0 else scores[place] + value
+
     for chunk in range(chunks):
-        for step in range(1, narrow):
-            made_copy(chunk, z, other(z, step, narrow)).wait_recv()
-        width = narrow * rows
-
-        def score(block, unused, chunk=chunk, width=width):
-            train = stack_rows([held[chunk, source] for source in range(narrow)])
-            scores[block, :, chunk * width : (chunk + 1) * width] = lax.dot_general(
-                gathered[block], train, ROW_BY_ROW, preferred_element_type=jnp.float32
-            )
-            return unused
-
-        lax.fori_loop(0, wide, score, 0)
-
-    for step in range(1, narrow):
-        share_copy(other(z, step, narrow), z).start()
+        for piece in range(pieces_out):
+            for step in range(1, narrow):
+                made_copy(chunk, piece, z, other(z, step, narrow)).wait_recv()
+            if chunk == chunks - 1 and piece == pieces_out - 1:
+                for step in range(half):
+                    block = far(step)
+                    score(chunk, piece, block)
+                    coarse[step] = scores[block].astype(jnp.bfloat16)
+                    coarse_copy(step, lax.rem(z, half)).start()
+                for step in range(1, half):
+                    block = near(step)
+                    score(chunk, piece, block)
+                    share_copy(block, z).start()
+                score(chunk, piece, z)
+            else:
+
+                def every(block, unused, chunk=chunk, piece=piece):
+                    score(chunk, piece, block)
+                    return unused
+
+                lax.fori_loop(0, wide, every, 0)
+
     span = jnp.broadcast_to(span_ref[pl.ds(w, 1), :], (8, span_ref.shape[1]))
     lane = lax.broadcasted_iota(jnp.int32, span.shape, 1)
     row_count = span.shape[1]
     total = scores[z]
-    for step in range(1, narrow):
-        source = other(z, step, narrow)
+    for step in range(1, half):
+        source = near(step)
         share_copy(z, source).wait_recv()
         total = total + shares[source]
+    for slot in range(half):
+        coarse_copy(0, slot).wait_recv()
+        total = total + coarse_in[slot].astype(jnp.float32)
 
     distance = 1
     while distance < min(SPAN_MOST, row_count):
@@ -292,15 +342,20 @@
     for chunk in range(chunks):
         for step in range(1, narrow):
             rows_copy(chunk, other(z, step, narrow), z).wait_send()
-            made_copy(chunk, other(z, step, narrow), z).wait_send()
+            for piece in range(pieces_out):
+                made_copy(chunk, piece, other(z, step, narrow), z).wait_send()
     for step in range(1, chips):
         there = other(chip, step, chips)
         grad_copy(there, w).wait_send()
         pass_copy(there, there * CORES + core).wait_send()
     own_pass(w).wait_send()
     for step in range(1, narrow):
-        share_copy(other(z, step, narrow), z).wait_send()
         peak_copy(other(z, step, narrow), w).wait_send()
+
+    for step in range(1, half):
+        share_copy(near(step), z).wait_send()
+    for step in range(half):
+        coarse_copy(step, lax.rem(z, half)).wait_send()
 
     @pl.when(w != z)
     def _():
@@ -320,6 +375,7 @@
         peer_rows = train_rows // narrow
         chunks = max(1, peer_rows // 16)
         rows = peer_rows // chunks
+        pieces = 2 if width % 512 == 0 else 1
         doc_share = DOCS_DEV * wide // narrow
         group_slots = -(-(cands * wide // NBEST) // 128) * 128
         in_vmem = pl.BlockSpec(memory_space=pltpu.VMEM)
@@ -342,18 +398,23 @@
                 pltpu.VMEM((wide, cands, width), jnp.bfloat16),
                 pltpu.VMEM((wide, cands, train_rows), jnp.float32),
                 pltpu.VMEM((narrow, cands, train_rows), jnp.float32),
+                pltpu.VMEM((chunks, narrow, rows, width), jnp.bfloat16),
+                pltpu.VMEM((narrow // 2, cands, train_rows), jnp.bfloat16),
+                pltpu.VMEM((narrow // 2, cands, train_rows), jnp.bfloat16),
                 pltpu.VMEM((narrow, doc_share, cands), jnp.float32),
                 pltpu.VMEM((wide, doc_share, cands), jnp.float32),
                 pltpu.VMEM((wide, doc_share, group_slots), jnp.float32),
                 dma((chunks, narrow)),
                 dma((chunks, narrow)),
-                dma((chunks, narrow)),
-                dma((chunks, narrow)),
+                dma((chunks, pieces, narrow)),
+                dma((chunks, pieces, narrow)),
                 dma((wide // CORES,)),
                 dma((wide // CORES,)),
                 dma((wide,)),
                 dma((narrow,)),
                 dma((narrow,)),
+                dma((narrow // 2,)),
+                dma((narrow // 2,)),
                 dma((narrow,)),
                 dma((wide,)),
                 dma((wide,)),

time: 74.6 us -> 68.6 us (0.920)
  Pallas kernels: 73 us -> 67 us
    pallas_call x1, Pallas kernels: 73 us -> 67 us  [local(): pl.pallas_call(functools.partial(kernel, chunks), out_shape=jax.ShapeDtyp...]
where the time goes in v3:
time: 68.6 us; the launch traced here: 68.4 us
  Pallas kernels  67 us (98%)
  local copies, waits for them, and re-layouts  1.32 us (2%)
    pallas_call x1, Pallas kernels, local(): pl.pallas_call(functools.partial(kernel, chunks), out_shape=jax.ShapeDtyp...  67 us

profile of v3, /device:TPU:0, one launch (start us, length us, event | category | flops | bytes accessed | tf_op | source)
XLA Modules:
  0.0 68.4 jit_solution(12708750858871419617)
XLA Ops:
  0.0 67.0 %shard_map.73 = f32[16,160]{1,0:T(8,128)} custom-call(bf16[2,4,16,4096]{3,2,1,0:T(8,128)(2,1)} %bitcast.4, bf16[160,4096]{1,0:T(8,128)(2,1)} %g_ref.1, s32[4,128]{1,0:T(4,128)} %bitcast.6, s32[1,160]{1,0:T(1,128)} %bitcast.7, f32[128,128]{1,0:T(8,128)} %eig_hbm.1, f32[128,128]{1,0:T(8,128)} %in_hbm.1, f32[128,128]{1,0:T(8,128)} %basis_hbm.1), custom_call_target="tpu_custom_call" | custom-call | tf_op jit(solution)/shard_map/pallas_call | solution.py:384
  67.1 1.3 %copy.9 = f32[160,16]{0,1:T(8,128)} copy(f32[160,16]{0,1:T(8,128)} %bitcast.5) | data formatting | bytes 20480

commit v4 on v3

--- a/solution.py
+++ b/solution.py
@@ -26,6 +26,18 @@
 
 def product(left, right):
     return jnp.dot(left, right, preferred_element_type=jnp.float32)
+
+
+def thirds(value, picks, dimensions):
+    high, rest = split(value)
+    middle = value - high.astype(jnp.float32)
+    low = (middle - rest.astype(jnp.float32)).astype(jnp.bfloat16)
+    terms = lax.dot_general(
+        jnp.concatenate([high, rest, low], axis=0), picks, dimensions,
+        preferred_element_type=jnp.float32,
+    )
+    count = value.shape[0]
+    return terms[:count] + terms[count : 2 * count] + terms[2 * count :]
 
 
 def stack_rows(pieces):
@@ -103,6 +115,8 @@
     def far(step):
         return far_base + lax.rem(z + step, half)
 
+    peers = [far(step) for step in range(half)] + [near(step) for step in range(1, half)]
+
     def coarse_copy(step, slot):
         return remote(
             coarse.at[step], coarse_in.at[slot], c_send.at[step], c_recv.at[slot],
@@ -130,8 +144,6 @@
             )
         )
     ]
-    for fetch in fetches:
-        fetch.start()
     barrier = pltpu.get_barrier_semaphore()
     for step in range(1, narrow):
         pl.semaphore_signal(
@@ -143,22 +155,22 @@
         pl.semaphore_signal(
             barrier, inc=1, device_id={"wide": peer, "narrow": w}, device_id_type=MESH
         )
-    pl.semaphore_wait(barrier, narrow - 1 + wide - 1 + jnp.where(w == z, 0, narrow))
-
     own_rows = [
         pltpu.make_async_copy(t_ref.at[chunk, z], taken.at[chunk, z], t_local.at[chunk])
         for chunk in range(chunks)
     ]
     own_grads = pltpu.make_async_copy(g_ref, gathered.at[w], g_local)
+    for copy in own_rows + fetches + [own_grads]:
+        copy.start()
+    pl.semaphore_wait(barrier, narrow - 1 + wide - 1 + jnp.where(w == z, 0, narrow))
+
     for chunk in range(chunks):
-        for step in range(1, narrow):
-            rows_copy(chunk, other(z, step, narrow), z).start()
-        own_rows[chunk].start()
+        for peer in peers:
+            rows_copy(chunk, peer, z).start()
         if chunk == 0:
             for step in range(1, chips):
                 grad_copy(other(chip, step, chips), w).start()
             own_pass(w).start()
-            own_grads.start()
 
     for fetch in fetches:
         fetch.wait()
@@ -220,8 +232,8 @@
             rows_copy(chunk, z, other(z, step, narrow)).wait_recv()
         precondition(chunk)
         for piece in range(pieces_out):
-            for step in range(1, narrow):
-                made_copy(chunk, piece, other(z, step, narrow), z).start()
+            for peer in peers:
+                made_copy(chunk, piece, peer, z).start()
         held[chunk, z] = made[chunk, z]
 
     for step in range(1, chips):
@@ -270,6 +282,16 @@
 
                 lax.fori_loop(0, wide, every, 0)
 
+    for chunk in range(chunks):
+        for step in range(1, narrow):
+            rows_copy(chunk, other(z, step, narrow), z).wait_send()
+            for piece in range(pieces_out):
+                made_copy(chunk, piece, other(z, step, narrow), z).wait_send()
+    for step in range(1, chips):
+        there = other(chip, step, chips)
+        grad_copy(there, w).wait_send()
+        pass_copy(there, there * CORES + core).wait_send()
+    own_pass(w).wait_send()
     span = jnp.broadcast_to(span_ref[pl.ds(w, 1), :], (8, span_ref.shape[1]))
     lane = lax.broadcasted_iota(jnp.int32, span.shape, 1)
     row_count = span.shape[1]
@@ -310,11 +332,15 @@
     def _():
         peaks_in[w] = peaks_out[z]
 
+    for step in range(1, half):
+        share_copy(near(step), z).wait_send()
+    for step in range(half):
+        coarse_copy(step, lax.rem(z, half)).wait_send()
     group_slots = sums.shape[2]
     cands = group_ref.shape[1]
     member = (
         group_ref[...] == lax.broadcasted_iota(jnp.int32, (group_slots, cands), 0)
-    ).astype(jnp.float32)
+    ).astype(jnp.bfloat16)
     for step in range(1, wide):
         peak_copy(z, other(w, step, wide)).wait_recv()
 
@@ -325,9 +351,7 @@
     doc_peak = peaks_in[0]
     for index in range(1, wide):
         doc_peak = jnp.maximum(doc_peak, peaks_in[index])
-    sums[w] = lax.dot_general(
-        doc_peak, member, ROW_BY_ROW, precision=HIGHEST, preferred_element_type=jnp.float32
-    )
+    sums[w] = thirds(doc_peak, member, ROW_BY_ROW)
     for step in range(1, wide):
         sum_copy(other(w, step, wide), w).start()
     for step in range(1, wide):
@@ -335,27 +359,11 @@
     mean = sums[0]
     for index in range(1, wide):
         mean = mean + sums[index]
-    out_ref[...] = doc_peak - jnp.dot(
-        mean * (1.0 / NBEST), member, precision=HIGHEST, preferred_element_type=jnp.float32
-    )
-
-    for chunk in range(chunks):
-        for step in range(1, narrow):
-            rows_copy(chunk, other(z, step, narrow), z).wait_send()
-            for piece in range(pieces_out):
-                made_copy(chunk, piece, other(z, step, narrow), z).wait_send()
-    for step in range(1, chips):
-        there = other(chip, step, chips)
-        grad_copy(there, w).wait_send()
-        pass_copy(there, there * CORES + core).wait_send()
-    own_pass(w).wait_send()
+    out_ref[...] = doc_peak - thirds(mean * (1.0 / NBEST), member, (((1,), (0,)), ((), ())))
+
     for step in range(1, narrow):
         peak_copy(other(z, step, narrow), w).wait_send()
 
-    for step in range(1, half):
-        share_copy(near(step), z).wait_send()
-    for step in range(half):
-        coarse_copy(step, lax.rem(z, half)).wait_send()
 
     @pl.when(w != z)
     def _():

time: 68.6 us -> 68.4 us (level)
  no operation moved by 1% of the time
where the time goes in v4:
time: 68.4 us; the launch traced here: 68.1 us
  Pallas kernels  66.8 us (98%)
  local copies, waits for them, and re-layouts  1.32 us (2%)
    pallas_call x1, Pallas kernels, local(): pl.pallas_call(functools.partial(kernel, chunks), out_shape=jax.ShapeDtyp...  66.8 us

profile of v4, /device:TPU:0, one launch (start us, length us, event | category | flops | bytes accessed | tf_op | source)
XLA Modules:
  0.0 68.1 jit_solution(17164772582336046094)
XLA Ops:
  0.0 66.8 %shard_map.73 = f32[16,160]{1,0:T(8,128)} custom-call(bf16[2,4,16,4096]{3,2,1,0:T(8,128)(2,1)} %bitcast.4, bf16[160,4096]{1,0:T(8,128)(2,1)} %g_ref.1, s32[4,128]{1,0:T(4,128)} %bitcast.6, s32[1,160]{1,0:T(1,128)} %bitcast.7, f32[128,128]{1,0:T(8,128)} %eig_hbm.1, f32[128,128]{1,0:T(8,128)} %in_hbm.1, f32[128,128]{1,0:T(8,128)} %basis_hbm.1), custom_call_target="tpu_custom_call" | custom-call | tf_op jit(solution)/shard_map/pallas_call | solution.py:392
  66.8 1.3 %copy.9 = f32[160,16]{0,1:T(8,128)} copy(f32[160,16]{0,1:T(8,128)} %bitcast.5) | data formatting | bytes 20480
